TPU v7x, 32 devices: a whole 2x2x4 slice. The times are simulated.
32 devices in a mesh: dp: 8 (over z, y), tp: 4 (over x, core).
Axes of the slice: x: 2, y: 2, z: 4, core: 2. Of those that a mesh axis runs over, the one named last changes fastest.
Arguments:
- queries: bfloat16 [2, 8, 8192], P(None, 'dp', 'tp'), may hold values from -8 to 8
- new_token_keys: bfloat16 [2, 8, 512], P(None, 'dp', 'tp'), may hold values from -6 to 6
- new_token_values: bfloat16 [2, 8, 512], P(None, 'dp', 'tp'), may hold values from -6 to 6
- key_pool: bfloat16 [512, 128, 512], P('dp', None, 'tp'), may hold values from -8 to 8
- value_pool: bfloat16 [512, 128, 512], P('dp', None, 'tp'), may hold values from -6 to 6
- block_list: int32 [2, 256, 2], P(None, ('dp', 'tp')), may hold values from 0 to 63, as said below
- context_len: int32 [2, 8], P(None, 'dp'), may hold values from 1 to 4096, as said below
Outputs:
- attn_out: bfloat16 [2, 8, 8192], P(None, 'dp', 'tp')
Inputs may be any that keep to these rules, and one draw needn't show every extreme that they name: `block_list`: each entry is (holder rank, pool slot). Every slot of every holder holds exactly one block of one micro-batch. On one holder, the blocks of one rank's requests over both micro-batches number 0 or 8; the bound 8 is also reached within a single micro-batch. Cached tokens, the new token aside. For every rank and micro-batch, ceil(context_len / 128) summed over the rank's 1 request is 32.
All inputs are finite; a program needn't handle non-finite values.
Results may differ from a plain program's by a relative error of at most 0.011.
Values may be sent and summed in bfloat16 or wider, within the bound.
A program may use at most 64 MiB of HBM per device.

v0:
```python
from functools import partial

import jax
import jax.numpy as jnp
from jax import lax
from jax.sharding import PartitionSpec as P


def block_terms(query_row_list, key_row_list, value_row_list, live_tokens):
    score_scale = query_row_list.shape[-1] ** (-0.5)
    scores = (
        jnp.einsum("ehd,ebd->ehb", query_row_list, key_row_list, preferred_element_type=jnp.float32)
        * score_scale
    )
    live_mask = (
        lax.broadcasted_iota(jnp.int32, scores.shape, 2)
        < jnp.maximum(live_tokens, 1)[:, None, None]
    )
    scores = jnp.where(live_mask, scores, -1e30)
    peak_score = jnp.max(scores, axis=2)
    weight = jnp.where(live_mask, jnp.exp(scores - peak_score[:, :, None]), 0.0)
    weight_sum = jnp.sum(weight, axis=2)
    mixed_sum = jnp.einsum(
        "ehb,ebd->ehd",
        weight.astype(jnp.bfloat16),
        value_row_list,
        preferred_element_type=jnp.float32,
    )
    return ((mixed_sum / weight_sum[:, :, None]).astype(jnp.bfloat16), peak_score, weight_sum)


def block_requests(block_rows, lengths, block_len):
    block_count = block_rows.shape[0]
    sizes_of = (lengths + block_len - 1) // block_len
    block_ends = jnp.cumsum(sizes_of)
    block_starts = block_ends - sizes_of
    position = jnp.arange(block_count, dtype=jnp.int32)
    request = jnp.sum((position[:, None] >= block_ends[None, :]).astype(jnp.int32), axis=1)
    chosen = request[:, None] == jnp.arange(lengths.shape[0], dtype=jnp.int32)[None, :]
    first_block = jnp.sum(jnp.where(chosen, block_starts[None, :], 0), axis=1)
    span_tokens = jnp.sum(jnp.where(chosen, lengths[None, :], 0), axis=1)
    return (request, jnp.clip(span_tokens - (position - first_block) * block_len, 0, block_len))


def slot_layout(block_all, lens_all, members, my_rank, slot_count, block_len, row_count):
    spread = lens_all.shape[1] // row_count
    group_rows = len(members) * row_count
    slot_ids = jnp.arange(slot_count, dtype=jnp.int32)
    slot_row = jnp.zeros((slot_count,), jnp.int32)
    slot_live = jnp.zeros((slot_count,), jnp.int32)
    slot_hits = jnp.zeros((slot_count,), jnp.int32)
    finder = partial(block_requests, block_len=block_len)
    for offset, index in enumerate(members):
        blocks = block_all[index].reshape(spread, -1, 2)
        request, live = jax.vmap(finder)(blocks, lens_all[index].reshape(spread, row_count))
        owner_ids = lax.broadcasted_iota(jnp.int32, request.shape, 0)
        target = owner_ids * group_rows + offset * row_count + request
        match = (blocks[:, :, 0] == my_rank)[:, :, None] & (
            blocks[:, :, 1][:, :, None] == slot_ids[None, None, :]
        )
        slot_row = slot_row + jnp.sum(jnp.where(match, target[:, :, None], 0), axis=(0, 1))
        slot_live = slot_live + jnp.sum(jnp.where(match, live[:, :, None], 0), axis=(0, 1))
        slot_hits = slot_hits + jnp.sum(match.astype(jnp.int32), axis=(0, 1))
    return (slot_row, slot_live, slot_hits > 0)


def per_device(
    queries, new_token_keys, new_token_values, key_pool, value_pool, block_list, context_len
):
    spread = lax.axis_size("dp")
    micro_count, row_count, feature_width = queries.shape
    slot_count, block_len, head_dim = key_pool.shape
    head_count = feature_width // head_dim
    block_table = lax.all_gather(block_list, "tp", axis=1, tiled=True)
    query_head_rows = queries.reshape(micro_count, row_count, head_count, head_dim)
    block_all, lens_all = (
        lax.all_gather(block_table, "dp", axis=1, tiled=True),
        lax.all_gather(context_len, "dp", axis=1, tiled=True),
    )
    my_rank = lax.axis_index("dp")
    rounds = [list(range(micro_count))]
    results = []
    for members in rounds:
        stacked = query_head_rows.reshape(len(members) * row_count, feature_width)
        group_rows = len(members) * row_count
        rows_total = spread * group_rows
        score_scale = head_dim ** (-0.5)
        everyone = lax.all_gather(stacked, "dp", axis=0, tiled=True)
        slot_row, slot_live, active = slot_layout(
            block_all, lens_all, members, my_rank, slot_count, block_len, row_count
        )
        asked = jnp.take(everyone, slot_row, axis=0).reshape(slot_count, head_count, head_dim)
        partial_out, peak_score, weight_sum = block_terms(asked, key_pool, value_pool, slot_live)
        onehot = (slot_row[None, :] == jnp.arange(rows_total, dtype=jnp.int32)[:, None]) & active[
            None, :
        ]
        local_peak = jnp.max(jnp.where(onehot[:, :, None], peak_score[None], -1e30), axis=1)
        key_row_list = new_token_keys.reshape(group_rows, head_dim)
        value_row_list = new_token_values.reshape(group_rows, head_dim)
        own_score = (
            jnp.einsum(
                "rhd,rd->rh",
                stacked.reshape(group_rows, head_count, head_dim),
                key_row_list,
                preferred_element_type=jnp.float32,
            )
            * score_scale
        )
        own_full = jnp.where(
            jnp.arange(spread, dtype=jnp.int32)[:, None, None] == my_rank, own_score[None], -1e30
        ).reshape(rows_total, head_count)
        ceiling_all = lax.pmax(jnp.maximum(local_peak, own_full), "dp")
        slot_ceiling = jnp.take(ceiling_all, slot_row, axis=0)
        slot_weight = jnp.where(
            active[:, None], jnp.exp(peak_score - slot_ceiling) * weight_sum, 0.0
        )
        selector = onehot.astype(jnp.float32)
        weighted = (slot_weight[:, :, None] * partial_out.astype(jnp.float32)).reshape(
            slot_count, feature_width
        )
        numer_all = jnp.dot(selector, weighted, precision=lax.Precision.HIGHEST)
        denom_all = jnp.dot(selector, slot_weight, precision=lax.Precision.HIGHEST)
        numer_mine, denom_mine = (
            lax.psum_scatter(
                numer_all.reshape(spread, group_rows, feature_width),
                "dp",
                scatter_dimension=0,
                tiled=True,
            ),
            lax.psum_scatter(
                denom_all.reshape(spread, group_rows, head_count),
                "dp",
                scatter_dimension=0,
                tiled=True,
            ),
        )
        ceiling_mine = lax.dynamic_index_in_dim(
            ceiling_all.reshape(spread, group_rows, head_count), my_rank, 0, keepdims=False
        )
        self_weight = jnp.exp(own_score - ceiling_mine)
        numerator = numer_mine.reshape(group_rows, head_count, head_dim) + self_weight[
            :, :, None
        ] * value_row_list[:, None, :].astype(jnp.float32)
        denominator = denom_mine.reshape(group_rows, head_count) + self_weight
        merged = (
            (numerator / denominator[:, :, None])
            .astype(jnp.bfloat16)
            .reshape(group_rows, feature_width)
        )
        for offset in range(len(members)):
            results.append(merged[offset * row_count : (offset + 1) * row_count])
        continue
    return jnp.stack(results)


def solution(mesh):
    placed = (
        P(None, "dp", "tp"),
        P(None, "dp", "tp"),
        P(None, "dp", "tp"),
        P("dp", None, "tp"),
        P("dp", None, "tp"),
        P(None, ("dp", "tp"), None),
        P(None, "dp"),
    )
    return jax.shard_map(
        per_device, mesh=mesh, in_specs=placed, out_specs=P(None, "dp", "tp"), check_vma=False
    )
```

profile of v0, /device:TPU:0, one launch (start us, length us, event | category | flops | bytes accessed | tf_op | source)
XLA Modules:
  0.0 200.2 jit_solution(9197749313719961478)
XLA Ops:
  6.5 0.0 copy-start
  6.5 0.0 copy-start.1
  6.5 0.0 all-reduce.4.cloned.1.call-start
  6.5 22.4 %all-gather.1 = s32[8,1,2]{2,1,0:T(1,128)S(1)} all-gather(s32[1,1,2]{2,1,0:T(1,128)} %bitcast.84), channel_id=1, replica_groups=mesh['dp'=8,'tp'=4] {'dp'}, dimensions={0}, use_global_device_ids=true | all-gather | bytes 72 | tf_op jit(solution)/shard_map/all_gather | solution.py:78
  29.0 0.1 copy.22
  29.1 0.8 copy.20
  29.9 5.2 %all_gather.12 = s32[2,32,2]{2,0,1:T(2,128)S(1)} all-gather(s32[2,8,2]{2,0,1:T(2,128)S(1)} %copy.20), channel_id=1, replica_groups=mesh['dp'=8,'tp'=4] {'tp'}, dimensions={1}, use_global_device_ids=true | all-gather | bytes 640 | tf_op jit(solution)/shard_map/all_gather | solution.py:74
  35.1 30.8 %all_gather.13 = s32[2,256,2]{2,0,1:T(2,128)S(1)} all-gather(s32[2,32,2]{2,0,1:T(2,128)S(1)} %all_gather.12), channel_id=1, replica_groups=mesh['dp'=8,'tp'=4] {'dp'}, dimensions={1}, use_global_device_ids=true | all-gather | bytes 4608 | tf_op jit(solution)/shard_map/all_gather | solution.py:77
  65.9 0.2 fusion.32
  66.1 0.1 fusion.34
  66.2 0.1 copy.32
  66.3 0.1 fusion.33
  66.4 0.1 copy.34
  66.5 0.1 copy.35
  66.6 0.1 copy.33
  66.8 0.1 convert_add_fusion
  66.9 0.2 convert_reduce_fusion
  67.1 0.2 convert_reduce_fusion.1
  67.4 0.0 copy-done.1
  67.4 30.5 %all-gather = bf16[16,1,2048]{2,1,0:T(2,128)(2,1)S(1)} all-gather(bf16[2,1,2048]{2,1,0:T(2,128)(2,1)S(1)} %copy.24), channel_id=2, replica_groups=mesh['dp'=8,'tp'=4] {'dp'}, dimensions={0}, use_global_device_ids=true | all-gather | bytes 73728 | tf_op jit(solution)/shard_map/all_gather | solution.py:88
  98.0 0.7 gather_fusion
  98.7 0.0 copy-start.2
  98.8 0.1 bitcast_select_fusion
  98.9 0.0 copy-done
  98.9 1.3 fusion.36
  100.2 0.1 copy.25
  100.3 0.1 broadcast_in_dim.186
  100.4 0.1 broadcast_in_dim.187
  100.5 0.0 copy-done.2
  100.5 0.1 fusion.14
  100.6 0.1 select_reduce_fusion
  100.7 0.1 select_maximum_fusion
  100.8 17.4 %pmax.7 = f32[16,16]{1,0:T(8,128)S(1)} all-reduce(f32[16,16]{1,0:T(8,128)S(1)} %select_maximum_fusion), channel_id=1, replica_groups=mesh['dp'=8,'tp'=4] {'dp'}, use_global_device_ids=true, to_apply=%region_8.9 | all-reduce | flops 256 | bytes 2048 | tf_op jit(solution)/shard_map/pmax | solution.py:112
  118.2 0.6 gather_fusion.1
  118.8 0.4 fusion.5
  119.2 0.1 multiply_select_fusion
  119.3 2.2 %fusion.3 = f32[64,16,128]{2,1,0:T(8,128)S(1)} fusion(bf16[64,128,128]{2,1,0:T(8,128)(2,1)} %param.11, f32[64,16,128]{2,1,0:T(8,128)S(1)} %get-tuple-element.32, f32[64,16]{1,0:T(8,128)S(1)} %fusion.5, f32[64,16]{1,0:T(8,128)S(1)} %multiply_select_fusion, f32[64,16]{1,0:T(8,128)S(1)} %get-tuple-element.31, s32[64]{0:T(128)S(1)} %add_maximum_fusion), kind=kOutput, calls=%fused_computation.7 | convolution fusion | flops 34603008 | bytes 3158272 | tf_op jit(solution)/shard_map/ehb,ebd->ehd/dot_general | solution.py:23
  121.5 0.0 copy-start.4
  121.5 0.0 copy-start.3
  121.5 0.1 reshape.554
  121.6 0.3 fusion.18
  121.9 0.8 copy.26
  122.7 0.0 all-reduce.4.cloned.1.call-update
  122.7 0.1 fusion.29
  122.8 19.5 %all-reduce.1 = f32[8,2,16]{2,1,0:T(2,128)S(1)} all-reduce(f32[8,2,16]{2,1,0:T(2,128)S(1)} %bitcast.76), channel_id=4, replica_groups=mesh['dp'=8,'tp'=4] {'dp'}, use_global_device_ids=true, to_apply=%region_11.12.clone | all-reduce | flops 256 | bytes 2048
  142.3 0.0 copy-done.4
  142.4 0.6 dynamic-slice
  142.9 0.7 fusion.24
  143.6 0.0 copy-done.3
  143.6 47.6 %all-reduce.4.cloned.1.call-done = f32[8,2,2048]{2,1,0:T(2,128)} async-done(((f32[8,2,2048]{2,1,0:T(2,128)}), f32[8,2,2048]{2,1,0:T(2,128)}) %all-reduce.4.cloned.1.call-update) | async-done | bytes 131088
  191.2 1.4 dynamic-slice_bitcast_fusion
  192.6 0.1 fusion.13
  192.7 0.6 pad_maximum_fusion
  (22 shorter events, 0.2 us)
Async XLA Ops:
  6.5 92.4 %copy-start = (bf16[64,128,128]{2,1,0:T(8,128)(2,1)S(1)}, bf16[64,128,128]{2,1,0:T(8,128)(2,1)}, u32[]{:S(2)}) copy-start(bf16[64,128,128]{2,1,0:T(8,128)(2,1)} %param.10) | copy-start | bytes 6291460
  6.5 60.8 %copy-start.1 = (bf16[2,1,2048]{2,0,1:T(2,128)(2,1)S(1)}, bf16[2,1,2048]{2,0,1:T(2,128)(2,1)}, u32[]{:S(2)}) copy-start(bf16[2,1,2048]{2,0,1:T(2,128)(2,1)} %param.7) | copy-start | bytes 24580
  6.5 184.7 %all-reduce.4.cloned.1.call-start = ((), (), s32[]{:S(2)}) async-start(), calls=%async_computation | async-start | bytes 262144
  98.7 1.7 copy-start.2
  121.5 20.8 %copy-start.4 = (u32[32]{0:T(128)S(1)}, u32[32]{0:T(128)}, u32[]{:S(2)}) copy-start(u32[32]{0:T(128)} %constant.100) | copy-start | bytes 388
  121.5 22.1 %copy-start.3 = (bf16[2,1,128]{2,0,1:T(2,128)(2,1)S(1)}, bf16[2,1,128]{2,0,1:T(2,128)(2,1)}, u32[]{:S(2)}) copy-start(bf16[2,1,128]{2,0,1:T(2,128)(2,1)} %param.9) | copy-start | bytes 1540
Sparse Core Ops, SparseCore 0:
  122.8 68.3 all-reduce.3
where the time goes:
time: 200 us
  blocking collectives  126 us (63%)
  waiting for transfers between devices  47.6 us (24%)
  between operations  13.7 us (7%)
  local copies, waits for them, and re-layouts  6.25 us (3%)
  matrix products  4 us (2%)
  other arithmetic  2.82 us (1%)
    unnamed x2, waiting for transfers between devices  47.6 us
    all_gather x1, blocking collectives, per_device(): lax.all_gather(block_table, 'dp', axis=1, tiled=True)  30.8 us
    all_gather x1, blocking collectives, per_device(): everyone = lax.all_gather(stacked, 'dp', axis=0, tiled=True)  30.5 us
    all_gather x1, blocking collectives, per_device(): lax.all_gather(context_len, 'dp', axis=1, tiled=True)  22.4 us
    unnamed x1, blocking collectives  19.5 us
    pmax x1, blocking collectives, per_device(): ceiling_all = lax.pmax(jnp.maximum(local_peak, own_full), 'dp')  17.4 us
    all_gather x1, blocking collectives, per_device(): block_table = lax.all_gather(block_list, 'tp', axis=1, tiled=True)  5.18 us
  transfers between devices with their start and end apart: 1, of which 1 were waited for; matrix products, arithmetic and copies ran while one was open for 1% of the time, Pallas kernels for 0%

commit v1 on v0

v1 whole, which is shorter than its diff:
```python
from functools import partial

import jax
import jax.numpy as jnp
from jax import lax
from jax.experimental import pallas as pl
from jax.experimental.pallas import tpu as pltpu
from jax.sharding import PartitionSpec as P

F32, BF16 = jnp.float32, jnp.bfloat16
LOW = -1e30
LANES = 128
RANK_CHUNK = 8
ROLLED_FROM = 64


def each(count, body):
    if count < ROLLED_FROM:
        for index in range(count):
            body(index)
    else:
        pl.loop(0, count)(body)


def iota(shape, axis):
    return lax.broadcasted_iota(jnp.int32, shape, axis)


def matmul(a, b):
    return jnp.dot(a, b, preferred_element_type=F32)


def kernel(
    ranks, shards, micro, heads,
    meta_ref, q_ref, new_k_ref, new_v_ref, k_hbm, v_hbm, out_ref,
    meta_all, q_all, k_vm, v_vm, pick, held, q_sel, scores, ceil_rep, acc_out, stat_out,
    acc_in, stat_in, kv_sem, send_sem, recv_sem,
):
    devices = ranks * shards
    slots, tokens, dim = k_vm.shape
    rows = micro * heads
    tall = slots * heads
    chunk_rows = RANK_CHUNK * rows
    chunks = ranks // RANK_CHUNK
    scale = dim ** (-0.5)
    rank, shard = lax.axis_index("dp"), lax.axis_index("tp")
    me = rank * shards + shard

    load_k = pltpu.make_async_copy(k_hbm, k_vm, kv_sem.at[0])
    load_v = pltpu.make_async_copy(v_hbm, v_vm, kv_sem.at[1])
    load_k.start()
    load_v.start()

    def device_at(step):
        other = lax.rem(me + step + 1, devices)
        return (other // shards, lax.rem(other, shards))

    def rank_at(step):
        return lax.rem(rank + step + 1, ranks)

    barrier = pltpu.get_barrier_semaphore()

    def greet(step):
        pl.semaphore_signal(
            barrier, inc=1, device_id=device_at(step), device_id_type=pl.DeviceIdType.MESH
        )

    each(devices - 1, greet)
    meta_all[me] = meta_ref[...]
    q_all[rank] = q_ref[...]
    pl.semaphore_wait(barrier, devices - 1)

    def send(src, dst, which, target):
        pltpu.make_async_remote_copy(
            src_ref=src, dst_ref=dst, send_sem=send_sem.at[which], recv_sem=recv_sem.at[which],
            device_id=target, device_id_type=pl.DeviceIdType.MESH,
        ).start()

    def drain(ref, sem, which, count):
        part = ref.at[pl.ds(0, count)]
        pltpu.make_async_copy(part, part, sem.at[which]).wait()

    each(devices - 1, lambda i: send(meta_all.at[me], meta_all.at[me], 0, device_at(i)))
    each(ranks - 1, lambda i: send(q_all.at[rank], q_all.at[rank], 1, (rank_at(i), shard)))

    lane = iota((1, LANES), 1)
    row_lane = lax.rem(iota((rows, LANES), 1), rows) == iota((rows, LANES), 0)
    spread = (iota((tall, slots), 0) // heads == iota((tall, slots), 1)).astype(F32).astype(BF16)
    spread_t = iota((slots, tall), 1) // heads == iota((slots, tall), 0)
    ones = jnp.ones((LANES, LANES), BF16)

    def per_head(ref):
        return jnp.concatenate(
            [jnp.broadcast_to(ref[m : m + 1, :].astype(F32), (heads, dim)) for m in range(micro)], 0
        )

    own = jnp.sum(q_ref[...].astype(F32) * per_head(new_k_ref), axis=1, keepdims=True) * scale
    own_row = jnp.sum(jnp.where(row_lane, own, 0.0), axis=0, keepdims=True)

    drain(meta_all, recv_sem, 0, devices - 1)
    entries = LANES // RANK_CHUNK
    slot_row = (rank * slots + iota((slots, LANES), 0)).astype(F32)
    half = entries // micro

    def find(group, carry):
        request, live = carry
        parts = meta_all[pl.ds(group * RANK_CHUNK, RANK_CHUNK)]
        both = jnp.sum(parts, axis=0)
        owner = (group * RANK_CHUNK + lane // entries) // shards
        name = (owner * micro + lax.rem(lane, entries) // half).astype(F32)
        match = jnp.broadcast_to(both[0:1], (slots, LANES)) == slot_row
        request = request + jnp.where(match, name, 0.0)
        live = live + jnp.where(match, both[1:2], 0.0)
        return request, live

    found = (jnp.zeros((slots, LANES), F32), jnp.zeros((slots, LANES), F32))
    groups = devices // RANK_CHUNK
    if groups < 16:
        for group in range(groups):
            found = find(group, found)
    else:
        found = lax.fori_loop(0, groups, find, found)
    summed = matmul(jnp.concatenate(found, axis=0).astype(BF16), ones)
    request = summed[:slots]
    wide = matmul(
        spread, jnp.concatenate([request, summed[slots:]], axis=1).astype(BF16)
    )
    request_tall, live_tall = wide[:, :LANES], wide[:, LANES:]
    target = request_tall * heads + lax.rem(iota((tall, LANES), 0), heads).astype(F32)
    target_row = jnp.sum(
        jnp.where(spread_t, jnp.concatenate([request] * (tall // LANES), axis=1), 0.0),
        axis=0, keepdims=True,
    ) * heads + lax.rem(iota((1, tall), 1), heads).astype(F32)

    def choose(c):
        for at in range(0, chunk_rows, LANES):
            column = (c * chunk_rows + at + iota((tall, LANES), 1)).astype(F32)
            pick[c, :, at : at + LANES] = jnp.where(target == column, 1.0, 0.0).astype(BF16)
        held[c] = jnp.where(
            (c * chunk_rows + iota((chunk_rows, tall), 0)).astype(F32) == target_row, 1.0, 0.0
        ).astype(BF16)

    each_chunk = lambda body: body(0) if chunks == 1 else pl.loop(0, chunks)(body)
    each_chunk(choose)

    drain(q_all, recv_sem, 1, ranks - 1)
    if chunks == 1:
        q_sel[...] = matmul(pick[0], q_all[...].reshape(chunk_rows, dim))
    else:
        q_sel[...] = jnp.zeros((tall, dim), F32)

        @pl.loop(0, chunks)
        def _(c):
            part = q_all[pl.ds(c * RANK_CHUNK, RANK_CHUNK)].reshape(chunk_rows, dim)
            q_sel[...] += matmul(pick[c], part)

    load_k.wait()
    batched = (((2,), (2,)), ((0,), (0,)))
    raw = lax.dot_general(
        q_sel[...].astype(BF16).reshape(slots, heads, dim), k_vm[...], batched,
        preferred_element_type=F32,
    ).reshape(tall, tokens) * scale
    alive = iota((tall, tokens), 1).astype(F32) < live_tall
    raw = jnp.where(alive, raw, LOW)
    scores[...] = raw
    peak = jnp.max(raw, axis=1, keepdims=True)

    def ceilings(c):
        name = (c * RANK_CHUNK * micro + iota((tall, LANES), 1)).astype(F32)
        best = jnp.where(request_tall == name, peak, LOW).reshape(slots, heads, LANES)
        best = jnp.max(best, axis=0).astype(BF16).astype(F32)
        top = jnp.concatenate(
            [
                jnp.broadcast_to(best[:, r : r + 1], (heads, LANES))
                for r in range(RANK_CHUNK * micro)
            ], 0,
        )
        stat_rows(c, 0, top)
        return top.astype(BF16)

    lane_slot = lax.rem(rank, LANES // rows) * rows

    def stat_rows(c, which, values):
        mine = iota((rows, LANES), 1) == iota((rows, LANES), 0) + lane_slot
        for o in range(RANK_CHUNK):
            part = jnp.where(mine, values[o * rows : (o + 1) * rows], 0.0)
            stat_out[c * RANK_CHUNK + o, which : which + 1] = jnp.sum(part, axis=0, keepdims=True)

    if chunks == 1:
        ceil_rep[...] = matmul(pick[0], ceilings(0))
    else:
        ceil_rep[...] = jnp.zeros((tall, LANES), F32)

        @pl.loop(0, chunks)
        def _(c):
            ceil_rep[...] += matmul(pick[c], ceilings(c))

    weight = jnp.exp(scores[...] - ceil_rep[...]).astype(BF16)
    total = matmul(weight, ones).astype(BF16)
    load_v.wait()
    mixed = lax.dot_general(
        weight.reshape(slots, heads, tokens), v_vm[...], (((2,), (1,)), ((0,), (0,))),
        preferred_element_type=F32,
    ).reshape(tall, dim).astype(BF16)
    both = jnp.concatenate([mixed, total], axis=1)

    def combine(c):
        merged = matmul(held[c], both)
        stat_rows(c, 1, merged[:, dim:])
        acc_out[pl.ds(c * RANK_CHUNK, RANK_CHUNK)] = (
            merged[:, :dim].astype(BF16).reshape(RANK_CHUNK, rows, dim)
        )

    each_chunk(combine)

    each(
        ranks - 1,
        lambda i: send(stat_out.at[rank_at(i)], stat_in.at[rank], 2, (rank_at(i), shard)),
    )
    each(
        ranks - 1,
        lambda i: send(acc_out.at[rank_at(i)], acc_in.at[rank], 3, (rank_at(i), shard)),
    )
    stat_in[rank] = stat_out[rank]
    acc_in[rank] = acc_out[rank]

    drain(stat_in, recv_sem, 2, ranks - 1)
    per_group = LANES // rows
    stats = [
        jnp.sum(stat_in[g : g + per_group], axis=0) for g in range(0, ranks, per_group)
    ]
    ceiling = own_row
    for both in stats:
        ceiling = jnp.maximum(ceiling, both[0:1])
    shift = LANES // 2
    while shift >= rows:
        ceiling = jnp.maximum(ceiling, pltpu.roll(ceiling, shift, 1))
        shift //= 2
    shares = [jnp.exp(both[0:1] - ceiling) for both in stats]
    bottom = sum(share * both[1:2] for share, both in zip(shares, stats))
    shift = LANES // 2
    while shift >= rows:
        bottom = bottom + pltpu.roll(bottom, shift, 1)
        shift //= 2
    own_share = jnp.exp(own_row - ceiling)
    inverse = 1.0 / (bottom + own_share)
    first = iota((rows, LANES), 1) == iota((rows, LANES), 0)
    own_column = jnp.sum(jnp.where(first, own_share * inverse, 0.0), axis=1, keepdims=True)
    result = own_column * per_head(new_v_ref)

    drain(acc_in, recv_sem, 3, ranks - 1)
    for g, share in enumerate(shares):
        factor = jnp.where(row_lane, share * inverse, 0.0)
        high = factor.astype(BF16)
        low = (factor - high.astype(F32)).astype(BF16)
        part = acc_in[g * per_group : (g + 1) * per_group].reshape(LANES, dim)
        result = result + matmul(high, part) + matmul(low, part)
    out_ref[...] = result.astype(BF16)

    drain(meta_all, send_sem, 0, devices - 1)
    drain(q_all, send_sem, 1, ranks - 1)
    drain(stat_out, send_sem, 2, ranks - 1)
    drain(acc_out, send_sem, 3, ranks - 1)


def per_device(
    ranks, shards, queries, new_token_keys, new_token_values, key_pool, value_pool, block_list, context_len
):
    micro, requests, width = queries.shape
    slots, tokens, dim = key_pool.shape
    heads = width // dim
    rows = micro * heads
    rank, shard = lax.axis_index("dp"), lax.axis_index("tp")
    me = rank * shards + shard
    listed = block_list.shape[1]
    position = shard * listed + jnp.arange(listed, dtype=jnp.int32)
    live = jnp.clip(context_len.reshape(micro, 1) - position[None, :] * tokens, 0, tokens)
    pool_row = block_list[:, :, 0] * slots + block_list[:, :, 1]
    entries = micro * listed
    meta = jnp.stack([pool_row.reshape(entries), live.reshape(entries)])
    place = jnp.arange(LANES, dtype=jnp.int32) // entries == lax.rem(me, LANES // entries)
    meta = jnp.where(place[None, :], jnp.tile(meta, (1, LANES // entries)), 0).astype(F32)
    tall = slots * heads
    chunks = ranks // RANK_CHUNK
    chunk_rows = RANK_CHUNK * rows
    vmem = pl.BlockSpec(memory_space=pltpu.VMEM)
    anywhere = pl.BlockSpec(memory_space=pl.ANY)
    out = pl.pallas_call(
        partial(kernel, ranks, shards, micro, heads),
        out_shape=jax.ShapeDtypeStruct((rows, dim), BF16),
        in_specs=[vmem, vmem, vmem, vmem, anywhere, anywhere],
        out_specs=vmem,
        scratch_shapes=[
            pltpu.VMEM((ranks * shards, 2, LANES), F32),
            pltpu.VMEM((ranks, rows, dim), BF16),
            pltpu.VMEM((slots, tokens, dim), BF16),
            pltpu.VMEM((slots, tokens, dim), BF16),
            pltpu.VMEM((chunks, tall, chunk_rows), BF16),
            pltpu.VMEM((chunks, chunk_rows, tall), BF16),
            pltpu.VMEM((tall, dim), F32),
            pltpu.VMEM((tall, tokens), F32),
            pltpu.VMEM((tall, LANES), F32),
            pltpu.VMEM((ranks, rows, dim), BF16),
            pltpu.VMEM((ranks, 2, LANES), F32),
            pltpu.VMEM((ranks, rows, dim), BF16),
            pltpu.VMEM((ranks, 2, LANES), F32),
            pltpu.SemaphoreType.DMA((2,)),
            pltpu.SemaphoreType.DMA((4,)),
            pltpu.SemaphoreType.DMA((4,)),
        ],
        compiler_params=pltpu.CompilerParams(
            collective_id=0, has_side_effects=True, vmem_limit_bytes=56 * 1024 * 1024
        ),
        name="paged_decode",
    )(
        meta,
        queries.reshape(rows, dim),
        new_token_keys.reshape(micro, dim),
        new_token_values.reshape(micro, dim),
        key_pool,
        value_pool,
    )
    return out.reshape(micro, requests, width)


def solution(mesh):
    placed = (
        P(None, "dp", "tp"),
        P(None, "dp", "tp"),
        P(None, "dp", "tp"),
        P("dp", None, "tp"),
        P("dp", None, "tp"),
        P(None, ("dp", "tp"), None),
        P(None, "dp"),
    )
    return jax.shard_map(
        partial(per_device, mesh.shape["dp"], mesh.shape["tp"]),
        mesh=mesh, in_specs=placed, out_specs=P(None, "dp", "tp"), check_vma=False,
    )
```

time: 200 us -> 26.3 us (0.13)
  blocking collectives: 126 us -> 0 us
  waiting for transfers between devices: 47.6 us -> 0 us
  Pallas kernels: 0 us -> 20.9 us
  between operations: 13.7 us -> 0.01 us
  matrix products: 4 us -> 0 us
  local copies, waits for them, and re-layouts: 6.25 us -> 2.87 us
    all_gather x4 -> x0, blocking collectives: 88.9 us -> none  [the longest x1 30.8 us: per_device(): lax.all_gather(block_table, 'dp', axis=1, tiled=True)]
    unnamed x2 -> x0, waiting for transfers between devices: 47.6 us -> none
    pallas_call x0 -> x1, Pallas kernels: none -> 20.9 us  [per_device(): pl.pallas_call(partial(kernel, ranks, shards, micro, heads), out_shape=ja...]
    unnamed x1 -> x0, blocking collectives: 19.5 us -> none
    pmax x1 -> x0, blocking collectives: 17.4 us -> none  [per_device(): ceiling_all = lax.pmax(jnp.maximum(local_peak, own_full), 'dp')]
    dot_general x5 -> x0, matrix products: 4 us -> none  [the longest x1 2.17 us: block_terms(): jnp.einsum('ehb,ebd->ehd', weight.astype(jnp.bfloat16), value_row_list, p...]
    unnamed x20 -> x0, local copies, waits for them, and re-layouts: 3.32 us -> none
    reshape x1 -> x2, local copies, waits for them, and re-layouts: 0.08 us -> 2.61 us  [the longest x1 1.31 us: per_device(): queries.reshape(rows, dim)]
  transfers between devices with their start and end apart: 1 -> 0, of which waited for: 1 -> 0; matrix products, arithmetic and copies ran while one was open for 1% -> 0% of each run, Pallas kernels for 0% -> 0%
where the time goes in v1:
time: 26.3 us; the launch traced here: 25.9 us
  Pallas kernels  20.9 us (79%)
  local copies, waits for them, and re-layouts  2.87 us (11%)
  other arithmetic  2.11 us (8%)
    pallas_call x1, Pallas kernels, per_device(): pl.pallas_call(partial(kernel, ranks, shards, micro, heads), out_shape=ja...  20.9 us
    reshape x1, local copies, waits for them, and re-layouts, per_device(): queries.reshape(rows, dim)  1.31 us
    reshape x1, local copies, waits for them, and re-layouts, per_device(): return out.reshape(micro, requests, width)  1.31 us
    add x1, other arithmetic, per_device(): pool_row = block_list[:, :, 0] * slots + block_list[:, :, 1]  0.78 us
    min x1, other arithmetic, per_device(): jnp.clip(context_len.reshape(micro, 1) - position[None, :] * tokens, 0, t...  0.73 us
    convert_element_type x1, other arithmetic, per_device(): jnp.where(place[None, :], jnp.tile(meta, (1, LANES // entries)), 0)  0.58 us

profile of v1, /device:TPU:0, one launch (start us, length us, event | category | flops | bytes accessed | tf_op | source)
XLA Modules:
  0.0 25.9 jit_solution(16424935386092849808)
XLA Ops:
  0.0 0.7 %subtract_clamp_fusion = s32[2,8]{1,0:T(2,128)S(1)} fusion(s32[8]{0:T(128)S(1)} %add_multiply_fusion, s32[2]{0:T(128)} %bitcast.5), kind=kLoop, calls=%fused_computation.3 | loop fusion | flops 32 | bytes 104 | tf_op jit(solution)/shard_map/jit(clip)/min | solution.py:277
  0.7 0.1 min.12
  0.8 0.8 %add_reduce_fusion = s32[2,8]{1,0:T(2,128)S(1)} fusion(s32[2,8,2]{1,2,0:T(2,128)} %param.12), kind=kLoop, calls=%fused_computation.4 | loop fusion | flops 32 | bytes 192 | tf_op jit(solution)/shard_map/add | solution.py:278
  1.6 0.1 add.33
  1.7 0.1 tile.10
  1.8 0.6 %select_convert_fusion.meta_ref = f32[2,128]{1,0:T(2,128)} fusion(s32[2,128]{1,0:T(2,128)S(1)} %tile.10, pred[128]{0:T(512)(128)(4,1)S(1)} %fusion), kind=kLoop, calls=%fused_computation.2 | loop fusion | flops 512 | bytes 2176 | tf_op jit(solution)/shard_map/convert_element_type | solution.py:282
  2.4 1.3 %reshape.87.q_ref = bf16[32,128]{1,0:T(8,128)(2,1)} reshape(bf16[2,1,2048]{2,0,1:T(2,128)(2,1)} %param.7) | data formatting | bytes 16384 | tf_op jit(solution)/shard_map/reshape | solution.py:317
  3.7 20.9 %paged_decode.1 = bf16[32,128]{1,0:T(8,128)(2,1)} custom-call(f32[2,128]{1,0:T(2,128)} %select_convert_fusion.meta_ref, bf16[32,128]{1,0:T(8,128)(2,1)} %reshape.87.q_ref, bf16[2,128]{1,0:T(2,128)(2,1)} %bitcast.6, bf16[2,128]{1,0:T(2,128)(2,1)} %bitcast.7, bf16[64,128,128]{2,1,0:T(8,128)(2,1)} %k_hbm.1, bf16[64,128,128]{2,1,0:T(8,128)(2,1)} %v_hbm.1), custom_call_target="tpu_custom_call" | custom-call | tf_op jit(solution)/shard_map/paged_decode/pallas_call | solution.py:288
  24.6 1.3 %reshape.90 = bf16[2,1,2048]{2,0,1:T(2,128)(2,1)} reshape(bf16[32,128]{1,0:T(8,128)(2,1)} %paged_decode.1) | data formatting | bytes 16384 | tf_op jit(solution)/shard_map/reshape | solution.py:323
  (4 shorter events, 0.0 us)

commit v2 on v1

--- a/solution.py
+++ b/solution.py
@@ -26,15 +26,25 @@
     return lax.broadcasted_iota(jnp.int32, shape, axis)
 
 
+def over(values, size):
+    if size & (size - 1):
+        return values // size
+    return lax.shift_right_logical(values, jnp.full_like(values, size.bit_length() - 1))
+
+
+def within(values, size):
+    return values - over(values, size) * size if size & (size - 1) else values & (size - 1)
+
+
 def matmul(a, b):
     return jnp.dot(a, b, preferred_element_type=F32)
 
 
 def kernel(
     ranks, shards, micro, heads,
-    meta_ref, q_ref, new_k_ref, new_v_ref, k_hbm, v_hbm, out_ref,
-    meta_all, q_all, k_vm, v_vm, pick, held, q_sel, scores, ceil_rep, acc_out, stat_out,
-    acc_in, stat_in, kv_sem, send_sem, recv_sem,
+    q_hbm, new_k_hbm, new_v_hbm, list_hbm, length_hbm, k_hbm, v_hbm, out_ref,
+    q_vm, new_k_vm, new_v_vm, list_vm, length_vm, meta_all, q_all, k_vm, v_vm, pick, held, q_sel, scores, ceil_rep, acc_out, stat_out,
+    acc_in, stat_in, load_sem, send_sem, recv_sem,
 ):
     devices = ranks * shards
     slots, tokens, dim = k_vm.shape
@@ -46,28 +56,79 @@
     rank, shard = lax.axis_index("dp"), lax.axis_index("tp")
     me = rank * shards + shard
 
-    load_k = pltpu.make_async_copy(k_hbm, k_vm, kv_sem.at[0])
-    load_v = pltpu.make_async_copy(v_hbm, v_vm, kv_sem.at[1])
-    load_k.start()
-    load_v.start()
-
-    def device_at(step):
-        other = lax.rem(me + step + 1, devices)
-        return (other // shards, lax.rem(other, shards))
+    def load(src, dst, which):
+        copy = pltpu.make_async_copy(src, dst, load_sem.at[which])
+        copy.start()
+        return copy
+
+    small = [
+        load(list_hbm, list_vm, 2), load(length_hbm, length_vm, 3), load(q_hbm, q_vm, 4),
+        load(new_k_hbm, new_k_vm, 5), load(new_v_hbm, new_v_vm, 6),
+    ]
+    load_k, load_v = load(k_hbm, k_vm, 0), load(v_hbm, v_vm, 1)
+
+    def after(here, step, size):
+        moved = here + step
+        return jnp.where(moved >= size, moved - size, moved)
 
     def rank_at(step):
-        return lax.rem(rank + step + 1, ranks)
+        return after(rank, step + 1, ranks)
+
+    shard_at = [shard] + [after(shard, step, shards) for step in range(1, shards)]
+
+    def everyone(body):
+        for other in shard_at[1:]:
+            body(rank, other)
+
+        def rank_body(step):
+            there = rank_at(step)
+            for other in shard_at:
+                body(there, other)
+
+        each(ranks - 1, rank_body)
 
     barrier = pltpu.get_barrier_semaphore()
 
-    def greet(step):
+    def greet(there, other):
         pl.semaphore_signal(
-            barrier, inc=1, device_id=device_at(step), device_id_type=pl.DeviceIdType.MESH
+            barrier, inc=1, device_id=(there, other), device_id_type=pl.DeviceIdType.MESH
         )
 
-    each(devices - 1, greet)
-    meta_all[me] = meta_ref[...]
-    q_all[rank] = q_ref[...]
+    everyone(greet)
+
+    lane = iota((1, LANES), 1)
+    listed = list_vm.shape[2]
+    entries = micro * listed
+    per_row = LANES // entries
+    offset = within(me, per_row) * entries
+    for copy in small:
+        copy.wait()
+    blank = jnp.zeros((1, LANES - listed), F32)
+    slot = within(lane, entries)
+    pool_rows = jnp.zeros((1, LANES), F32)
+    count = jnp.zeros((1, LANES), jnp.int32)
+    for m in range(micro):
+        listing = list_vm[m]
+        pool = (listing[0:1] * slots + listing[1:2]).astype(F32)
+        pool = jnp.concatenate([pool, blank], axis=1)
+        pool_rows = pool_rows + (pltpu.roll(pool, m * listed, 1) if m else pool)
+        position = shard * listed + slot - m * listed
+        left = jnp.clip(length_vm[0:1, m : m + 1] - position * tokens, 0, tokens)
+        count = jnp.where(over(slot, listed) == m, left, count)
+    width = entries
+    while width < LANES:
+        pool_rows = pool_rows + pltpu.roll(pool_rows, width, 1)
+        width *= 2
+    mine = (lane >= offset) & (lane < offset + entries)
+    meta_all[me, 0:1] = jnp.where(mine, pool_rows, 0.0)
+    meta_all[me, 1:2] = jnp.where(mine, count.astype(F32), 0.0)
+    q_wide = q_vm[0].astype(F32)
+    own_q = jnp.concatenate(
+        [
+            q_wide[m : m + 1, n * dim : (n + 1) * dim] for m in range(micro) for n in range(heads)
+        ], 0,
+    )
+    q_all[rank] = own_q.astype(BF16)
     pl.semaphore_wait(barrier, devices - 1)
 
     def send(src, dst, which, target):
@@ -80,41 +141,39 @@
         part = ref.at[pl.ds(0, count)]
         pltpu.make_async_copy(part, part, sem.at[which]).wait()
 
-    each(devices - 1, lambda i: send(meta_all.at[me], meta_all.at[me], 0, device_at(i)))
+    everyone(lambda there, other: send(meta_all.at[me], meta_all.at[me], 0, (there, other)))
     each(ranks - 1, lambda i: send(q_all.at[rank], q_all.at[rank], 1, (rank_at(i), shard)))
 
-    lane = iota((1, LANES), 1)
-    row_lane = lax.rem(iota((rows, LANES), 1), rows) == iota((rows, LANES), 0)
-    spread = (iota((tall, slots), 0) // heads == iota((tall, slots), 1)).astype(F32).astype(BF16)
-    spread_t = iota((slots, tall), 1) // heads == iota((slots, tall), 0)
+    row_lane = within(iota((rows, LANES), 1), rows) == iota((rows, LANES), 0)
+    spread = (over(iota((tall, slots), 0), heads) == iota((tall, slots), 1)).astype(F32).astype(BF16)
+    spread_t = over(iota((slots, tall), 1), heads) == iota((slots, tall), 0)
     ones = jnp.ones((LANES, LANES), BF16)
 
     def per_head(ref):
+        flat = ref[0].astype(F32)
         return jnp.concatenate(
-            [jnp.broadcast_to(ref[m : m + 1, :].astype(F32), (heads, dim)) for m in range(micro)], 0
+            [jnp.broadcast_to(flat[m : m + 1], (heads, dim)) for m in range(micro)], 0
         )
 
-    own = jnp.sum(q_ref[...].astype(F32) * per_head(new_k_ref), axis=1, keepdims=True) * scale
+    own = jnp.sum(own_q * per_head(new_k_vm), axis=1, keepdims=True) * scale
     own_row = jnp.sum(jnp.where(row_lane, own, 0.0), axis=0, keepdims=True)
 
     drain(meta_all, recv_sem, 0, devices - 1)
-    entries = LANES // RANK_CHUNK
     slot_row = (rank * slots + iota((slots, LANES), 0)).astype(F32)
-    half = entries // micro
 
     def find(group, carry):
         request, live = carry
-        parts = meta_all[pl.ds(group * RANK_CHUNK, RANK_CHUNK)]
+        parts = meta_all[pl.ds(group * per_row, per_row)]
         both = jnp.sum(parts, axis=0)
-        owner = (group * RANK_CHUNK + lane // entries) // shards
-        name = (owner * micro + lax.rem(lane, entries) // half).astype(F32)
+        owner = over(group * per_row + over(lane, entries), shards)
+        name = (owner * micro + over(within(lane, entries), listed)).astype(F32)
         match = jnp.broadcast_to(both[0:1], (slots, LANES)) == slot_row
         request = request + jnp.where(match, name, 0.0)
         live = live + jnp.where(match, both[1:2], 0.0)
         return request, live
 
     found = (jnp.zeros((slots, LANES), F32), jnp.zeros((slots, LANES), F32))
-    groups = devices // RANK_CHUNK
+    groups = devices // per_row
     if groups < 16:
         for group in range(groups):
             found = find(group, found)
@@ -126,11 +185,11 @@
         spread, jnp.concatenate([request, summed[slots:]], axis=1).astype(BF16)
     )
     request_tall, live_tall = wide[:, :LANES], wide[:, LANES:]
-    target = request_tall * heads + lax.rem(iota((tall, LANES), 0), heads).astype(F32)
+    target = request_tall * heads + within(iota((tall, LANES), 0), heads).astype(F32)
     target_row = jnp.sum(
         jnp.where(spread_t, jnp.concatenate([request] * (tall // LANES), axis=1), 0.0),
         axis=0, keepdims=True,
-    ) * heads + lax.rem(iota((1, tall), 1), heads).astype(F32)
+    ) * heads + within(iota((1, tall), 1), heads).astype(F32)
 
     def choose(c):
         for at in range(0, chunk_rows, LANES):
@@ -178,7 +237,7 @@
         stat_rows(c, 0, top)
         return top.astype(BF16)
 
-    lane_slot = lax.rem(rank, LANES // rows) * rows
+    lane_slot = within(rank, LANES // rows) * rows
 
     def stat_rows(c, which, values):
         mine = iota((rows, LANES), 1) == iota((rows, LANES), 0) + lane_slot
@@ -246,7 +305,7 @@
     inverse = 1.0 / (bottom + own_share)
     first = iota((rows, LANES), 1) == iota((rows, LANES), 0)
     own_column = jnp.sum(jnp.where(first, own_share * inverse, 0.0), axis=1, keepdims=True)
-    result = own_column * per_head(new_v_ref)
+    result = own_column * per_head(new_v_vm)
 
     drain(acc_in, recv_sem, 3, ranks - 1)
     for g, share in enumerate(shares):
@@ -255,7 +314,9 @@
         low = (factor - high.astype(F32)).astype(BF16)
         part = acc_in[g * per_group : (g + 1) * per_group].reshape(LANES, dim)
         result = result + matmul(high, part) + matmul(low, part)
-    out_ref[...] = result.astype(BF16)
+    for n in range(heads):
+        pair = [result[m * heads + n : m * heads + n + 1] for m in range(micro)]
+        out_ref[0, :, n * dim : (n + 1) * dim] = jnp.concatenate(pair, axis=0).astype(BF16)
 
     drain(meta_all, send_sem, 0, devices - 1)
     drain(q_all, send_sem, 1, ranks - 1)
@@ -270,16 +331,10 @@
     slots, tokens, dim = key_pool.shape
     heads = width // dim
     rows = micro * heads
-    rank, shard = lax.axis_index("dp"), lax.axis_index("tp")
-    me = rank * shards + shard
-    listed = block_list.shape[1]
-    position = shard * listed + jnp.arange(listed, dtype=jnp.int32)
-    live = jnp.clip(context_len.reshape(micro, 1) - position[None, :] * tokens, 0, tokens)
-    pool_row = block_list[:, :, 0] * slots + block_list[:, :, 1]
-    entries = micro * listed
-    meta = jnp.stack([pool_row.reshape(entries), live.reshape(entries)])
-    place = jnp.arange(LANES, dtype=jnp.int32) // entries == lax.rem(me, LANES // entries)
-    meta = jnp.where(place[None, :], jnp.tile(meta, (1, LANES // entries)), 0).astype(F32)
+    queries, new_token_keys, new_token_values = (
+        x.transpose(1, 0, 2) for x in (queries, new_token_keys, new_token_values)
+    )
+    block_list, context_len = block_list.transpose(0, 2, 1), context_len.transpose(1, 0)
     tall = slots * heads
     chunks = ranks // RANK_CHUNK
     chunk_rows = RANK_CHUNK * rows
@@ -287,10 +342,15 @@
     anywhere = pl.BlockSpec(memory_space=pl.ANY)
     out = pl.pallas_call(
         partial(kernel, ranks, shards, micro, heads),
-        out_shape=jax.ShapeDtypeStruct((rows, dim), BF16),
-        in_specs=[vmem, vmem, vmem, vmem, anywhere, anywhere],
+        out_shape=jax.ShapeDtypeStruct(queries.shape, BF16),
+        in_specs=[anywhere] * 7,
         out_specs=vmem,
         scratch_shapes=[
+            pltpu.VMEM(queries.shape, BF16),
+            pltpu.VMEM(new_token_keys.shape, BF16),
+            pltpu.VMEM(new_token_values.shape, BF16),
+            pltpu.VMEM(block_list.shape, jnp.int32),
+            pltpu.VMEM(context_len.shape, jnp.int32),
             pltpu.VMEM((ranks * shards, 2, LANES), F32),
             pltpu.VMEM((ranks, rows, dim), BF16),
             pltpu.VMEM((slots, tokens, dim), BF16),
@@ -304,7 +364,7 @@
             pltpu.VMEM((ranks, 2, LANES), F32),
             pltpu.VMEM((ranks, rows, dim), BF16),
             pltpu.VMEM((ranks, 2, LANES), F32),
-            pltpu.SemaphoreType.DMA((2,)),
+            pltpu.SemaphoreType.DMA((7,)),
             pltpu.SemaphoreType.DMA((4,)),
             pltpu.SemaphoreType.DMA((4,)),
         ],
@@ -313,14 +373,9 @@
         ),
         name="paged_decode",
     )(
-        meta,
-        queries.reshape(rows, dim),
-        new_token_keys.reshape(micro, dim),
-        new_token_values.reshape(micro, dim),
-        key_pool,
-        value_pool,
-    )
-    return out.reshape(micro, requests, width)
+        queries, new_token_keys, new_token_values, block_list, context_len, key_pool, value_pool
+    )
+    return out.transpose(1, 0, 2)
 
 
 def solution(mesh):

time: 26.3 us -> 21.8 us (0.83)
  other arithmetic: 2.11 us -> 0 us
  local copies, waits for them, and re-layouts: 2.87 us -> 1.3 us
  Pallas kernels: 20.9 us -> 20.3 us
    reshape x2 -> x0, local copies, waits for them, and re-layouts: 2.61 us -> none  [the longest x1 1.31 us: per_device(): queries.reshape(rows, dim)]
    unnamed x0 -> x1, local copies, waits for them, and re-layouts: none -> 1.3 us
    add x1 -> x0, other arithmetic: 0.78 us -> none  [per_device(): pool_row = block_list[:, :, 0] * slots + block_list[:, :, 1]]
    min x1 -> x0, other arithmetic: 0.73 us -> none  [per_device(): jnp.clip(context_len.reshape(micro, 1) - position[None, :] * tokens, 0, t...]
    pallas_call x1, Pallas kernels: 20.9 us -> 20.3 us  [per_device(): pl.pallas_call(partial(kernel, ranks, shards, micro, heads), out_shape=ja...]
    convert_element_type x1 -> x0, other arithmetic: 0.58 us -> none  [per_device(): jnp.where(place[None, :], jnp.tile(meta, (1, LANES // entries)), 0)]
where the time goes in v2:
time: 21.8 us; the launch traced here: 21.6 us
  Pallas kernels  20.3 us (93%)
  local copies, waits for them, and re-layouts  1.3 us (6%)
    pallas_call x1, Pallas kernels, per_device(): pl.pallas_call(partial(kernel, ranks, shards, micro, heads), out_shape=ja...  20.3 us
    unnamed x1, local copies, waits for them, and re-layouts  1.3 us

profile of v2, /device:TPU:0, one launch (start us, length us, event | category | flops | bytes accessed | tf_op | source)
XLA Modules:
  0.0 21.6 jit_solution(97435703231228380)
XLA Ops:
  0.0 20.3 %paged_decode.1 = bf16[1,2,2048]{2,1,0:T(2,128)(2,1)} custom-call(bf16[1,2,2048]{2,1,0:T(2,128)(2,1)} %bitcast.7, bf16[1,2,128]{2,1,0:T(2,128)(2,1)} %bitcast.9, bf16[1,2,128]{2,1,0:T(2,128)(2,1)} %bitcast.10, s32[2,2,8]{2,1,0:T(2,128)} %bitcast.8, s32[1,2]{1,0:T(1,128)} %bitcast.11, bf16[64,128,128]{2,1,0:T(8,128)(2,1)} %k_hbm.1, bf16[64,128,128]{2,1,0:T(8,128)(2,1)} %v_hbm.1), custom_call_target="tpu_custom_call" | custom-call | tf_op jit(solution)/shard_map/paged_decode/pallas_call | solution.py:343
  20.3 1.3 %copy.9 = bf16[2,1,2048]{2,0,1:T(2,128)(2,1)} copy(bf16[2,1,2048]{2,0,1:T(2,128)(2,1)} %bitcast.6) | data formatting | bytes 16384

commit v3 on v2

--- a/solution.py
+++ b/solution.py
@@ -11,6 +11,7 @@
 LOW = -1e30
 LANES = 128
 RANK_CHUNK = 8
+VMEM_BYTES = 52 << 20
 ROLLED_FROM = 64
 
 
@@ -43,7 +44,7 @@
 def kernel(
     ranks, shards, micro, heads,
     q_hbm, new_k_hbm, new_v_hbm, list_hbm, length_hbm, k_hbm, v_hbm, out_ref,
-    q_vm, new_k_vm, new_v_vm, list_vm, length_vm, meta_all, q_all, k_vm, v_vm, pick, held, q_sel, scores, ceil_rep, acc_out, stat_out,
+    q_vm, new_k_vm, new_v_vm, list_vm, length_vm, meta_all, q_all, k_vm, v_vm, pick, held, q_sel, ceil_rep, acc_out, stat_out,
     acc_in, stat_in, load_sem, send_sem, recv_sem,
 ):
     devices = ranks * shards
@@ -145,7 +146,6 @@
     each(ranks - 1, lambda i: send(q_all.at[rank], q_all.at[rank], 1, (rank_at(i), shard)))
 
     row_lane = within(iota((rows, LANES), 1), rows) == iota((rows, LANES), 0)
-    spread = (over(iota((tall, slots), 0), heads) == iota((tall, slots), 1)).astype(F32).astype(BF16)
     spread_t = over(iota((slots, tall), 1), heads) == iota((slots, tall), 0)
     ones = jnp.ones((LANES, LANES), BF16)
 
@@ -181,10 +181,12 @@
         found = lax.fori_loop(0, groups, find, found)
     summed = matmul(jnp.concatenate(found, axis=0).astype(BF16), ones)
     request = summed[:slots]
-    wide = matmul(
-        spread, jnp.concatenate([request, summed[slots:]], axis=1).astype(BF16)
-    )
-    request_tall, live_tall = wide[:, :LANES], wide[:, LANES:]
+    def heads_of(values):
+        return jnp.concatenate(
+            [jnp.broadcast_to(values[i : i + 1], (heads, LANES)) for i in range(slots)], 0
+        )
+
+    request_tall, live_tall = heads_of(request), heads_of(summed[slots:])
     target = request_tall * heads + within(iota((tall, LANES), 0), heads).astype(F32)
     target_row = jnp.sum(
         jnp.where(spread_t, jnp.concatenate([request] * (tall // LANES), axis=1), 0.0),
@@ -221,8 +223,14 @@
     ).reshape(tall, tokens) * scale
     alive = iota((tall, tokens), 1).astype(F32) < live_tall
     raw = jnp.where(alive, raw, LOW)
-    scores[...] = raw
     peak = jnp.max(raw, axis=1, keepdims=True)
+    weight = jnp.exp(raw - peak).astype(BF16)
+    total = matmul(weight, ones)
+    load_v.wait()
+    mixed = lax.dot_general(
+        weight.reshape(slots, heads, tokens), v_vm[...], (((2,), (1,)), ((0,), (0,))),
+        preferred_element_type=F32,
+    ).reshape(tall, dim)
 
     def ceilings(c):
         name = (c * RANK_CHUNK * micro + iota((tall, LANES), 1)).astype(F32)
@@ -254,14 +262,8 @@
         def _(c):
             ceil_rep[...] += matmul(pick[c], ceilings(c))
 
-    weight = jnp.exp(scores[...] - ceil_rep[...]).astype(BF16)
-    total = matmul(weight, ones).astype(BF16)
-    load_v.wait()
-    mixed = lax.dot_general(
-        weight.reshape(slots, heads, tokens), v_vm[...], (((2,), (1,)), ((0,), (0,))),
-        preferred_element_type=F32,
-    ).reshape(tall, dim).astype(BF16)
-    both = jnp.concatenate([mixed, total], axis=1)
+    rescale = jnp.exp(peak - ceil_rep[...])
+    both = jnp.concatenate([(mixed * rescale).astype(BF16), (total * rescale).astype(BF16)], axis=1)
 
     def combine(c):
         merged = matmul(held[c], both)
@@ -358,7 +360,6 @@
             pltpu.VMEM((chunks, tall, chunk_rows), BF16),
             pltpu.VMEM((chunks, chunk_rows, tall), BF16),
             pltpu.VMEM((tall, dim), F32),
-            pltpu.VMEM((tall, tokens), F32),
             pltpu.VMEM((tall, LANES), F32),
             pltpu.VMEM((ranks, rows, dim), BF16),
             pltpu.VMEM((ranks, 2, LANES), F32),
@@ -369,7 +370,7 @@
             pltpu.SemaphoreType.DMA((4,)),
         ],
         compiler_params=pltpu.CompilerParams(
-            collective_id=0, has_side_effects=True, vmem_limit_bytes=56 * 1024 * 1024
+            collective_id=0, has_side_effects=True, vmem_limit_bytes=VMEM_BYTES
         ),
         name="paged_decode",
     )(

time: 21.8 us -> 23.8 us (1.092)
  local copies, waits for them, and re-layouts: 1.3 us -> 3.94 us
  Pallas kernels: 20.3 us -> 19.6 us
    unnamed x1 -> x11, local copies, waits for them, and re-layouts: 1.3 us -> 3.94 us
    pallas_call x1, Pallas kernels: 20.3 us -> 19.6 us  [per_device(): pl.pallas_call(partial(kernel, ranks, shards, micro, heads), out_shape=ja...]
where the time goes in v3:
time: 23.8 us; the launch traced here: 23.5 us
  Pallas kernels  19.6 us (82%)
  local copies, waits for them, and re-layouts  3.94 us (17%)
    pallas_call x1, Pallas kernels, per_device(): pl.pallas_call(partial(kernel, ranks, shards, micro, heads), out_shape=ja...  19.6 us
    unnamed x11, local copies, waits for them, and re-layouts  3.94 us

profile of v3, /device:TPU:0, one launch (start us, length us, event | category | flops | bytes accessed | tf_op | source)
XLA Modules:
  0.0 23.5 jit_solution(3222606046602681924)
XLA Ops:
  0.0 0.0 copy-start
  0.0 0.7 %copy-done = bf16[2,1,2048]{2,0,1:T(2,128)(2,1)S(1)} copy-done((bf16[2,1,2048]{2,0,1:T(2,128)(2,1)S(1)}, bf16[2,1,2048]{2,0,1:T(2,128)(2,1)}, u32[]{:S(2)}) %copy-start) | copy-done | bytes 8216
  0.7 0.0 copy-start.1
  0.7 0.7 %copy-done.1 = s32[2,8,2]{1,2,0:T(2,128)S(1)} copy-done((s32[2,8,2]{1,2,0:T(2,128)S(1)}, s32[2,8,2]{1,2,0:T(2,128)}, u32[]{:S(2)}) %copy-start.1) | copy-done | bytes 152
  1.4 0.0 copy-start.2
  1.4 0.7 %copy-done.2 = bf16[2,1,128]{2,0,1:T(2,128)(2,1)S(1)} copy-done((bf16[2,1,128]{2,0,1:T(2,128)(2,1)S(1)}, bf16[2,1,128]{2,0,1:T(2,128)(2,1)}, u32[]{:S(2)}) %copy-start.2) | copy-done | bytes 536
  2.0 0.0 copy-start.3
  2.0 0.7 %copy-done.3 = bf16[2,1,128]{2,0,1:T(2,128)(2,1)S(1)} copy-done((bf16[2,1,128]{2,0,1:T(2,128)(2,1)S(1)}, bf16[2,1,128]{2,0,1:T(2,128)(2,1)}, u32[]{:S(2)}) %copy-start.3) | copy-done | bytes 536
  2.7 0.0 copy-start.4
  2.7 0.7 %copy-done.4 = s32[2,1]{0,1:T(1,128)S(1)} copy-done((s32[2,1]{0,1:T(1,128)S(1)}, s32[2,1]{0,1:T(1,128)}, u32[]{:S(2)}) %copy-start.4) | copy-done | bytes 32
  3.3 19.6 %paged_decode.1 = bf16[1,2,2048]{2,1,0:T(2,128)(2,1)S(1)} custom-call(bf16[1,2,2048]{2,1,0:T(2,128)(2,1)S(1)} %bitcast.7, bf16[1,2,128]{2,1,0:T(2,128)(2,1)S(1)} %bitcast.9, bf16[1,2,128]{2,1,0:T(2,128)(2,1)S(1)} %bitcast.10, s32[2,2,8]{2,1,0:T(2,128)S(1)} %bitcast.8, s32[1,2]{1,0:T(1,128)S(1)} %bitcast.11, bf16[64,128,128]{2,1,0:T(8,128)(2,1)} %k_hbm.1, ...), custom_call_target="tpu_custom_call" | custom-call | tf_op jit(solution)/shard_map/paged_decode/pallas_call | solution.py:345
  22.9 0.6 %copy.9 = bf16[2,1,2048]{2,0,1:T(2,128)(2,1)} copy(bf16[2,1,2048]{2,0,1:T(2,128)(2,1)S(1)} %bitcast.6) | data formatting | bytes 16384
Async XLA Ops:
  0.0 0.7 %copy-start = (bf16[2,1,2048]{2,0,1:T(2,128)(2,1)S(1)}, bf16[2,1,2048]{2,0,1:T(2,128)(2,1)}, u32[]{:S(2)}) copy-start(bf16[2,1,2048]{2,0,1:T(2,128)(2,1)} %param.7) | copy-start | bytes 24580
  0.7 0.7 %copy-start.1 = (s32[2,8,2]{1,2,0:T(2,128)S(1)}, s32[2,8,2]{1,2,0:T(2,128)}, u32[]{:S(2)}) copy-start(s32[2,8,2]{1,2,0:T(2,128)} %param.12) | copy-start | bytes 388
  1.4 0.7 %copy-start.2 = (bf16[2,1,128]{2,0,1:T(2,128)(2,1)S(1)}, bf16[2,1,128]{2,0,1:T(2,128)(2,1)}, u32[]{:S(2)}) copy-start(bf16[2,1,128]{2,0,1:T(2,128)(2,1)} %param.8) | copy-start | bytes 1540
  2.0 0.7 %copy-start.3 = (bf16[2,1,128]{2,0,1:T(2,128)(2,1)S(1)}, bf16[2,1,128]{2,0,1:T(2,128)(2,1)}, u32[]{:S(2)}) copy-start(bf16[2,1,128]{2,0,1:T(2,128)(2,1)} %param.9) | copy-start | bytes 1540
  2.7 0.7 %copy-start.4 = (s32[2,1]{0,1:T(1,128)S(1)}, s32[2,1]{0,1:T(1,128)}, u32[]{:S(2)}) copy-start(s32[2,1]{0,1:T(1,128)} %param.13) | copy-start | bytes 28

commit v4 on v3

--- a/solution.py
+++ b/solution.py
@@ -11,7 +11,7 @@
 LOW = -1e30
 LANES = 128
 RANK_CHUNK = 8
-VMEM_BYTES = 52 << 20
+VMEM_BYTES = 56 << 20
 ROLLED_FROM = 64
 
 
@@ -44,10 +44,9 @@
 def kernel(
     ranks, shards, micro, heads,
     q_hbm, new_k_hbm, new_v_hbm, list_hbm, length_hbm, k_hbm, v_hbm, out_ref,
-    q_vm, new_k_vm, new_v_vm, list_vm, length_vm, meta_all, q_all, k_vm, v_vm, pick, held, q_sel, ceil_rep, acc_out, stat_out,
+    q_vm, new_k_vm, new_v_vm, list_vm, length_vm, meta_own, meta_all, q_all, k_vm, v_vm, pick, held, q_sel, ceil_rep, acc_out, stat_out,
     acc_in, stat_in, load_sem, send_sem, recv_sem,
 ):
-    devices = ranks * shards
     slots, tokens, dim = k_vm.shape
     rows = micro * heads
     tall = slots * heads
@@ -77,16 +76,12 @@
 
     shard_at = [shard] + [after(shard, step, shards) for step in range(1, shards)]
 
-    def everyone(body):
+    def peers(body):
         for other in shard_at[1:]:
             body(rank, other)
 
-        def rank_body(step):
-            there = rank_at(step)
-            for other in shard_at:
-                body(there, other)
-
-        each(ranks - 1, rank_body)
+    def holders(body):
+        each(ranks - 1, lambda step: body(rank_at(step)))
 
     barrier = pltpu.get_barrier_semaphore()
 
@@ -95,7 +90,8 @@
             barrier, inc=1, device_id=(there, other), device_id_type=pl.DeviceIdType.MESH
         )
 
-    everyone(greet)
+    holders(lambda there: greet(there, shard))
+    peers(greet)
 
     lane = iota((1, LANES), 1)
     listed = list_vm.shape[2]
@@ -121,8 +117,8 @@
         pool_rows = pool_rows + pltpu.roll(pool_rows, width, 1)
         width *= 2
     mine = (lane >= offset) & (lane < offset + entries)
-    meta_all[me, 0:1] = jnp.where(mine, pool_rows, 0.0)
-    meta_all[me, 1:2] = jnp.where(mine, count.astype(F32), 0.0)
+    meta_own[shard, 0:1] = jnp.where(mine, pool_rows, 0.0)
+    meta_own[shard, 1:2] = jnp.where(mine, count.astype(F32), 0.0)
     q_wide = q_vm[0].astype(F32)
     own_q = jnp.concatenate(
         [
@@ -130,7 +126,7 @@
         ], 0,
     )
     q_all[rank] = own_q.astype(BF16)
-    pl.semaphore_wait(barrier, devices - 1)
+    pl.semaphore_wait(barrier, ranks - 1 + shards - 1)
 
     def send(src, dst, which, target):
         pltpu.make_async_remote_copy(
@@ -142,8 +138,11 @@
         part = ref.at[pl.ds(0, count)]
         pltpu.make_async_copy(part, part, sem.at[which]).wait()
 
-    everyone(lambda there, other: send(meta_all.at[me], meta_all.at[me], 0, (there, other)))
-    each(ranks - 1, lambda i: send(q_all.at[rank], q_all.at[rank], 1, (rank_at(i), shard)))
+    peers(lambda there, other: send(meta_own.at[shard], meta_own.at[shard], 4, (there, other)))
+    holders(lambda there: send(q_all.at[rank], q_all.at[rank], 1, (there, shard)))
+    drain(meta_own, recv_sem, 4, shards - 1)
+    meta_all[rank] = jnp.sum(meta_own[...], axis=0)
+    holders(lambda there: send(meta_all.at[rank], meta_all.at[rank], 0, (there, shard)))
 
     row_lane = within(iota((rows, LANES), 1), rows) == iota((rows, LANES), 0)
     spread_t = over(iota((slots, tall), 1), heads) == iota((slots, tall), 0)
@@ -158,12 +157,12 @@
     own = jnp.sum(own_q * per_head(new_k_vm), axis=1, keepdims=True) * scale
     own_row = jnp.sum(jnp.where(row_lane, own, 0.0), axis=0, keepdims=True)
 
-    drain(meta_all, recv_sem, 0, devices - 1)
+    drain(meta_all, recv_sem, 0, ranks - 1)
     slot_row = (rank * slots + iota((slots, LANES), 0)).astype(F32)
 
     def find(group, carry):
         request, live = carry
-        parts = meta_all[pl.ds(group * per_row, per_row)]
+        parts = meta_all[pl.ds(group * share, share)]
         both = jnp.sum(parts, axis=0)
         owner = over(group * per_row + over(lane, entries), shards)
         name = (owner * micro + over(within(lane, entries), listed)).astype(F32)
@@ -173,7 +172,8 @@
         return request, live
 
     found = (jnp.zeros((slots, LANES), F32), jnp.zeros((slots, LANES), F32))
-    groups = devices // per_row
+    share = per_row // shards
+    groups = ranks // share
     if groups < 16:
         for group in range(groups):
             found = find(group, found)
@@ -274,14 +274,8 @@
 
     each_chunk(combine)
 
-    each(
-        ranks - 1,
-        lambda i: send(stat_out.at[rank_at(i)], stat_in.at[rank], 2, (rank_at(i), shard)),
-    )
-    each(
-        ranks - 1,
-        lambda i: send(acc_out.at[rank_at(i)], acc_in.at[rank], 3, (rank_at(i), shard)),
-    )
+    holders(lambda there: send(stat_out.at[there], stat_in.at[rank], 2, (there, shard)))
+    holders(lambda there: send(acc_out.at[there], acc_in.at[rank], 3, (there, shard)))
     stat_in[rank] = stat_out[rank]
     acc_in[rank] = acc_out[rank]
 
@@ -320,7 +314,8 @@
         pair = [result[m * heads + n : m * heads + n + 1] for m in range(micro)]
         out_ref[0, :, n * dim : (n + 1) * dim] = jnp.concatenate(pair, axis=0).astype(BF16)
 
-    drain(meta_all, send_sem, 0, devices - 1)
+    drain(meta_own, send_sem, 4, shards - 1)
+    drain(meta_all, send_sem, 0, ranks - 1)
     drain(q_all, send_sem, 1, ranks - 1)
     drain(stat_out, send_sem, 2, ranks - 1)
     drain(acc_out, send_sem, 3, ranks - 1)
@@ -344,7 +339,7 @@
     anywhere = pl.BlockSpec(memory_space=pl.ANY)
     out = pl.pallas_call(
         partial(kernel, ranks, shards, micro, heads),
-        out_shape=jax.ShapeDtypeStruct(queries.shape, BF16),
+        out_shape=pltpu.VMEM(queries.shape, BF16),
         in_specs=[anywhere] * 7,
         out_specs=vmem,
         scratch_shapes=[
@@ -353,7 +348,8 @@
             pltpu.VMEM(new_token_values.shape, BF16),
             pltpu.VMEM(block_list.shape, jnp.int32),
             pltpu.VMEM(context_len.shape, jnp.int32),
-            pltpu.VMEM((ranks * shards, 2, LANES), F32),
+            pltpu.VMEM((shards, 2, LANES), F32),
+            pltpu.VMEM((ranks, 2, LANES), F32),
             pltpu.VMEM((ranks, rows, dim), BF16),
             pltpu.VMEM((slots, tokens, dim), BF16),
             pltpu.VMEM((slots, tokens, dim), BF16),
@@ -366,8 +362,8 @@
             pltpu.VMEM((ranks, rows, dim), BF16),
             pltpu.VMEM((ranks, 2, LANES), F32),
             pltpu.SemaphoreType.DMA((7,)),
-            pltpu.SemaphoreType.DMA((4,)),
-            pltpu.SemaphoreType.DMA((4,)),
+            pltpu.SemaphoreType.DMA((5,)),
+            pltpu.SemaphoreType.DMA((5,)),
         ],
         compiler_params=pltpu.CompilerParams(
             collective_id=0, has_side_effects=True, vmem_limit_bytes=VMEM_BYTES

time: 23.8 us -> 21.8 us (0.916)
  local copies, waits for them, and re-layouts: 3.94 us -> 0.6 us
  Pallas kernels: 19.6 us -> 21 us
    unnamed x11 -> x1, local copies, waits for them, and re-layouts: 3.94 us -> 0.6 us
    pallas_call x1, Pallas kernels: 19.6 us -> 21 us  [per_device(): pl.pallas_call(partial(kernel, ranks, shards, micro, heads), out_shape=pl...]
where the time goes in v4:
time: 21.8 us; the launch traced here: 21.7 us
  Pallas kernels  21 us (96%)
  local copies, waits for them, and re-layouts  0.6 us (3%)
    pallas_call x1, Pallas kernels, per_device(): pl.pallas_call(partial(kernel, ranks, shards, micro, heads), out_shape=pl...  21 us
    unnamed x1, local copies, waits for them, and re-layouts  0.6 us

profile of v4, /device:TPU:0, one launch (start us, length us, event | category | flops | bytes accessed | tf_op | source)
XLA Modules:
  0.0 21.7 jit_solution(9778425950620244358)
XLA Ops:
  0.0 21.0 %paged_decode.1 = bf16[1,2,2048]{2,1,0:T(2,128)(2,1)S(1)} custom-call(bf16[1,2,2048]{2,1,0:T(2,128)(2,1)} %bitcast.7, bf16[1,2,128]{2,1,0:T(2,128)(2,1)} %bitcast.9, bf16[1,2,128]{2,1,0:T(2,128)(2,1)} %bitcast.10, s32[2,2,8]{2,1,0:T(2,128)} %bitcast.8, s32[1,2]{1,0:T(1,128)} %bitcast.11, bf16[64,128,128]{2,1,0:T(8,128)(2,1)} %k_hbm.1, ...), custom_call_target="tpu_custom_call" | custom-call | tf_op jit(solution)/shard_map/paged_decode/pallas_call | solution.py:340
  21.1 0.6 %copy.9 = bf16[2,1,2048]{2,0,1:T(2,128)(2,1)} copy(bf16[2,1,2048]{2,0,1:T(2,128)(2,1)S(1)} %bitcast.6) | data formatting | bytes 16384

commit v5 on v3

--- a/solution.py
+++ b/solution.py
@@ -11,7 +11,7 @@
 LOW = -1e30
 LANES = 128
 RANK_CHUNK = 8
-VMEM_BYTES = 52 << 20
+VMEM_BYTES = 56 << 20
 ROLLED_FROM = 64
 
 
@@ -96,6 +96,9 @@
         )
 
     everyone(greet)
+
+    def holders(body):
+        each(ranks - 1, lambda step: body(rank_at(step)))
 
     lane = iota((1, LANES), 1)
     listed = list_vm.shape[2]
@@ -143,7 +146,7 @@
         pltpu.make_async_copy(part, part, sem.at[which]).wait()
 
     everyone(lambda there, other: send(meta_all.at[me], meta_all.at[me], 0, (there, other)))
-    each(ranks - 1, lambda i: send(q_all.at[rank], q_all.at[rank], 1, (rank_at(i), shard)))
+    holders(lambda there: send(q_all.at[rank], q_all.at[rank], 1, (there, shard)))
 
     row_lane = within(iota((rows, LANES), 1), rows) == iota((rows, LANES), 0)
     spread_t = over(iota((slots, tall), 1), heads) == iota((slots, tall), 0)
@@ -216,19 +219,31 @@
             q_sel[...] += matmul(pick[c], part)
 
     load_k.wait()
-    batched = (((2,), (2,)), ((0,), (0,)))
-    raw = lax.dot_general(
-        q_sel[...].astype(BF16).reshape(slots, heads, dim), k_vm[...], batched,
+    pairs = slots // 2
+    crossed = lax.dot_general(
+        q_sel[...].astype(BF16).reshape(pairs, 2 * heads, dim),
+        k_vm[...].reshape(pairs, 2 * tokens, dim),
+        (((2,), (2,)), ((0,), (0,))),
         preferred_element_type=F32,
-    ).reshape(tall, tokens) * scale
+    )
+    raw = jnp.stack([crossed[:, :heads, :tokens], crossed[:, heads:, tokens:]], axis=1)
+    raw = raw.reshape(tall, tokens) * scale
     alive = iota((tall, tokens), 1).astype(F32) < live_tall
     raw = jnp.where(alive, raw, LOW)
     peak = jnp.max(raw, axis=1, keepdims=True)
     weight = jnp.exp(raw - peak).astype(BF16)
     total = matmul(weight, ones)
     load_v.wait()
+    paired = weight.reshape(pairs, 2, heads, tokens)
+    nothing = jnp.zeros((pairs, heads, tokens), BF16)
+    diagonal = jnp.concatenate(
+        [
+            jnp.concatenate([paired[:, 0], nothing], axis=2),
+            jnp.concatenate([nothing, paired[:, 1]], axis=2),
+        ], 1,
+    )
     mixed = lax.dot_general(
-        weight.reshape(slots, heads, tokens), v_vm[...], (((2,), (1,)), ((0,), (0,))),
+        diagonal, v_vm[...].reshape(pairs, 2 * tokens, dim), (((2,), (1,)), ((0,), (0,))),
         preferred_element_type=F32,
     ).reshape(tall, dim)
 
@@ -274,14 +289,8 @@
 
     each_chunk(combine)
 
-    each(
-        ranks - 1,
-        lambda i: send(stat_out.at[rank_at(i)], stat_in.at[rank], 2, (rank_at(i), shard)),
-    )
-    each(
-        ranks - 1,
-        lambda i: send(acc_out.at[rank_at(i)], acc_in.at[rank], 3, (rank_at(i), shard)),
-    )
+    holders(lambda there: send(stat_out.at[there], stat_in.at[rank], 2, (there, shard)))
+    holders(lambda there: send(acc_out.at[there], acc_in.at[rank], 3, (there, shard)))
     stat_in[rank] = stat_out[rank]
     acc_in[rank] = acc_out[rank]
 
@@ -344,7 +353,7 @@
     anywhere = pl.BlockSpec(memory_space=pl.ANY)
     out = pl.pallas_call(
         partial(kernel, ranks, shards, micro, heads),
-        out_shape=jax.ShapeDtypeStruct(queries.shape, BF16),
+        out_shape=pltpu.VMEM(queries.shape, BF16),
         in_specs=[anywhere] * 7,
         out_specs=vmem,
         scratch_shapes=[

time: 23.8 us -> 19.8 us (0.83)
  local copies, waits for them, and re-layouts: 3.94 us -> 0.6 us
  Pallas kernels: 19.6 us -> 19 us
    unnamed x11 -> x1, local copies, waits for them, and re-layouts: 3.94 us -> 0.6 us
    pallas_call x1, Pallas kernels: 19.6 us -> 19 us  [per_device(): pl.pallas_call(partial(kernel, ranks, shards, micro, heads), out_shape=pl...]
where the time goes in v5:
time: 19.8 us; the launch traced here: 19.6 us
  Pallas kernels  19 us (96%)
  local copies, waits for them, and re-layouts  0.6 us (3%)
    pallas_call x1, Pallas kernels, per_device(): pl.pallas_call(partial(kernel, ranks, shards, micro, heads), out_shape=pl...  19 us
    unnamed x1, local copies, waits for them, and re-layouts  0.6 us

profile of v5, /device:TPU:0, one launch (start us, length us, event | category | flops | bytes accessed | tf_op | source)
XLA Modules:
  0.0 19.6 jit_solution(13665067417504259371)
XLA Ops:
  0.0 19.0 %paged_decode.1 = bf16[1,2,2048]{2,1,0:T(2,128)(2,1)S(1)} custom-call(bf16[1,2,2048]{2,1,0:T(2,128)(2,1)} %bitcast.7, bf16[1,2,128]{2,1,0:T(2,128)(2,1)} %bitcast.9, bf16[1,2,128]{2,1,0:T(2,128)(2,1)} %bitcast.10, s32[2,2,8]{2,1,0:T(2,128)} %bitcast.8, s32[1,2]{1,0:T(1,128)} %bitcast.11, bf16[64,128,128]{2,1,0:T(8,128)(2,1)} %k_hbm.1, ...), custom_call_target="tpu_custom_call" | custom-call | tf_op jit(solution)/shard_map/paged_decode/pallas_call | solution.py:354
  19.0 0.6 %copy.9 = bf16[2,1,2048]{2,0,1:T(2,128)(2,1)} copy(bf16[2,1,2048]{2,0,1:T(2,128)(2,1)S(1)} %bitcast.6) | data formatting | bytes 16384

commit v6 on v5

--- a/solution.py
+++ b/solution.py
@@ -103,8 +103,9 @@
     lane = iota((1, LANES), 1)
     listed = list_vm.shape[2]
     entries = micro * listed
-    per_row = LANES // entries
-    offset = within(me, per_row) * entries
+    span = 2 * entries
+    per_row = LANES // span
+    offset = within(me, per_row) * span
     for copy in small:
         copy.wait()
     blank = jnp.zeros((1, LANES - listed), F32)
@@ -123,9 +124,10 @@
     while width < LANES:
         pool_rows = pool_rows + pltpu.roll(pool_rows, width, 1)
         width *= 2
-    mine = (lane >= offset) & (lane < offset + entries)
-    meta_all[me, 0:1] = jnp.where(mine, pool_rows, 0.0)
-    meta_all[me, 1:2] = jnp.where(mine, count.astype(F32), 0.0)
+    first = within(lane, span) < entries
+    mine = (lane >= offset) & (lane < offset + span)
+    both = jnp.where(first, pool_rows, count.astype(F32))
+    meta_all[me] = jnp.where(mine, both, 0.0)
     q_wide = q_vm[0].astype(F32)
     own_q = jnp.concatenate(
         [
@@ -168,11 +170,11 @@
         request, live = carry
         parts = meta_all[pl.ds(group * per_row, per_row)]
         both = jnp.sum(parts, axis=0)
-        owner = over(group * per_row + over(lane, entries), shards)
-        name = (owner * micro + over(within(lane, entries), listed)).astype(F32)
-        match = jnp.broadcast_to(both[0:1], (slots, LANES)) == slot_row
+        owner = over(group * per_row + over(lane, span), shards)
+        name = (owner * micro + over(within(lane, span), listed)).astype(F32)
+        match = jnp.broadcast_to(jnp.where(first, both, -1.0), (slots, LANES)) == slot_row
         request = request + jnp.where(match, name, 0.0)
-        live = live + jnp.where(match, both[1:2], 0.0)
+        live = live + jnp.where(match, pltpu.roll(both, LANES - entries, 1), 0.0)
         return request, live
 
     found = (jnp.zeros((slots, LANES), F32), jnp.zeros((slots, LANES), F32))
@@ -196,13 +198,18 @@
         axis=0, keepdims=True,
     ) * heads + within(iota((1, tall), 1), heads).astype(F32)
 
+    one, zero = jnp.ones((), BF16), jnp.zeros((), BF16)
+    row_name = iota((chunk_rows, LANES), 0).astype(F32).astype(BF16)
+
     def choose(c):
+        base = jnp.asarray(c * chunk_rows, jnp.int32).astype(F32)
+        wanted = (target - base).astype(BF16)
         for at in range(0, chunk_rows, LANES):
-            column = (c * chunk_rows + at + iota((tall, LANES), 1)).astype(F32)
-            pick[c, :, at : at + LANES] = jnp.where(target == column, 1.0, 0.0).astype(BF16)
-        held[c] = jnp.where(
-            (c * chunk_rows + iota((chunk_rows, tall), 0)).astype(F32) == target_row, 1.0, 0.0
-        ).astype(BF16)
+            column = jnp.broadcast_to((lane + at).astype(F32).astype(BF16), (tall, LANES))
+            pick[c, :, at : at + LANES] = jnp.where(wanted == column, one, zero)
+        for at in range(0, tall, LANES):
+            here = jnp.broadcast_to(target_row[:, at : at + LANES] - base, (chunk_rows, LANES))
+            held[c, :, at : at + LANES] = jnp.where(here.astype(BF16) == row_name, one, zero)
 
     each_chunk = lambda body: body(0) if chunks == 1 else pl.loop(0, chunks)(body)
     each_chunk(choose)
@@ -314,8 +321,8 @@
         shift //= 2
     own_share = jnp.exp(own_row - ceiling)
     inverse = 1.0 / (bottom + own_share)
-    first = iota((rows, LANES), 1) == iota((rows, LANES), 0)
-    own_column = jnp.sum(jnp.where(first, own_share * inverse, 0.0), axis=1, keepdims=True)
+    head_lane = iota((rows, LANES), 1) == iota((rows, LANES), 0)
+    own_column = jnp.sum(jnp.where(head_lane, own_share * inverse, 0.0), axis=1, keepdims=True)
     result = own_column * per_head(new_v_vm)
 
     drain(acc_in, recv_sem, 3, ranks - 1)
@@ -362,7 +369,7 @@
             pltpu.VMEM(new_token_values.shape, BF16),
             pltpu.VMEM(block_list.shape, jnp.int32),
             pltpu.VMEM(context_len.shape, jnp.int32),
-            pltpu.VMEM((ranks * shards, 2, LANES), F32),
+            pltpu.VMEM((ranks * shards, 1, LANES), F32),
             pltpu.VMEM((ranks, rows, dim), BF16),
             pltpu.VMEM((slots, tokens, dim), BF16),
             pltpu.VMEM((slots, tokens, dim), BF16),

time: 19.8 us -> 19.5 us (0.985)
  Pallas kernels: 19 us -> 18.8 us
    pallas_call x1, Pallas kernels: 19 us -> 18.8 us  [per_device(): pl.pallas_call(partial(kernel, ranks, shards, micro, heads), out_shape=pl...]
where the time goes in v6:
time: 19.5 us; the launch traced here: 19.4 us
  Pallas kernels  18.8 us (96%)
  local copies, waits for them, and re-layouts  0.6 us (3%)
    pallas_call x1, Pallas kernels, per_device(): pl.pallas_call(partial(kernel, ranks, shards, micro, heads), out_shape=pl...  18.8 us
    unnamed x1, local copies, waits for them, and re-layouts  0.6 us

profile of v6, /device:TPU:0, one launch (start us, length us, event | category | flops | bytes accessed | tf_op | source)
XLA Modules:
  0.0 19.4 jit_solution(1495361211724213675)
XLA Ops:
  0.0 18.8 %paged_decode.1 = bf16[1,2,2048]{2,1,0:T(2,128)(2,1)S(1)} custom-call(bf16[1,2,2048]{2,1,0:T(2,128)(2,1)} %bitcast.7, bf16[1,2,128]{2,1,0:T(2,128)(2,1)} %bitcast.9, bf16[1,2,128]{2,1,0:T(2,128)(2,1)} %bitcast.10, s32[2,2,8]{2,1,0:T(2,128)} %bitcast.8, s32[1,2]{1,0:T(1,128)} %bitcast.11, bf16[64,128,128]{2,1,0:T(8,128)(2,1)} %k_hbm.1, ...), custom_call_target="tpu_custom_call" | custom-call | tf_op jit(solution)/shard_map/paged_decode/pallas_call | solution.py:361
  18.8 0.6 %copy.9 = bf16[2,1,2048]{2,0,1:T(2,128)(2,1)} copy(bf16[2,1,2048]{2,0,1:T(2,128)(2,1)S(1)} %bitcast.6) | data formatting | bytes 16384

commit v7 on v6

--- a/solution.py
+++ b/solution.py
@@ -226,33 +226,46 @@
             q_sel[...] += matmul(pick[c], part)
 
     load_k.wait()
-    pairs = slots // 2
-    crossed = lax.dot_general(
-        q_sel[...].astype(BF16).reshape(pairs, 2 * heads, dim),
-        k_vm[...].reshape(pairs, 2 * tokens, dim),
-        (((2,), (2,)), ((0,), (0,))),
-        preferred_element_type=F32,
-    )
-    raw = jnp.stack([crossed[:, :heads, :tokens], crossed[:, heads:, tokens:]], axis=1)
-    raw = raw.reshape(tall, tokens) * scale
+    quads = slots // 4
+
+    def placed(values):
+        part = values.reshape(quads, 4, heads, LANES)
+        nothing = jnp.zeros((quads, heads, LANES), BF16)
+        rows_of = [(part[:, 0], nothing), (part[:, 2], nothing), (nothing, part[:, 1]), (nothing, part[:, 3])]
+        return jnp.concatenate([jnp.concatenate(pair, axis=2) for pair in rows_of], axis=1)
+
+    def square(values, order):
+        part = values.reshape(quads, 4, LANES, LANES)
+        block = [part[:, i] for i in order]
+        upper, lower = jnp.concatenate(block[:2], axis=2), jnp.concatenate(block[2:], axis=2)
+        return jnp.concatenate([upper, lower], axis=1)
+
+    def useful(values):
+        left, right = values[:, :, :LANES], values[:, :, LANES:]
+        pieces = [
+            left[:, :heads], left[:, 2 * heads : 3 * heads],
+            right[:, heads : 2 * heads], right[:, 3 * heads :],
+        ]
+        return jnp.stack(pieces, axis=1).reshape(tall, LANES)
+
+    raw = useful(
+        lax.dot_general(
+            placed(q_sel[...].astype(BF16)), square(k_vm[...], (0, 1, 2, 3)),
+            (((2,), (2,)), ((0,), (0,))), preferred_element_type=F32,
+        )
+    ) * scale
     alive = iota((tall, tokens), 1).astype(F32) < live_tall
     raw = jnp.where(alive, raw, LOW)
     peak = jnp.max(raw, axis=1, keepdims=True)
     weight = jnp.exp(raw - peak).astype(BF16)
     total = matmul(weight, ones)
     load_v.wait()
-    paired = weight.reshape(pairs, 2, heads, tokens)
-    nothing = jnp.zeros((pairs, heads, tokens), BF16)
-    diagonal = jnp.concatenate(
-        [
-            jnp.concatenate([paired[:, 0], nothing], axis=2),
-            jnp.concatenate([nothing, paired[:, 1]], axis=2),
-        ], 1,
-    )
-    mixed = lax.dot_general(
-        diagonal, v_vm[...].reshape(pairs, 2 * tokens, dim), (((2,), (1,)), ((0,), (0,))),
-        preferred_element_type=F32,
-    ).reshape(tall, dim)
+    mixed = useful(
+        lax.dot_general(
+            placed(weight), square(v_vm[...], (0, 2, 1, 3)),
+            (((2,), (1,)), ((0,), (0,))), preferred_element_type=F32,
+        )
+    )
 
     def ceilings(c):
         name = (c * RANK_CHUNK * micro + iota((tall, LANES), 1)).astype(F32)

time: 19.5 us -> 19.5 us (level)
  no operation moved by 1% of the time
where the time goes in v7:
time: 19.5 us; the launch traced here: 19.3 us
  Pallas kernels  18.7 us (96%)
  local copies, waits for them, and re-layouts  0.6 us (3%)
    pallas_call x1, Pallas kernels, per_device(): pl.pallas_call(partial(kernel, ranks, shards, micro, heads), out_shape=pl...  18.7 us
    unnamed x1, local copies, waits for them, and re-layouts  0.6 us

profile of v7, /device:TPU:0, one launch (start us, length us, event | category | flops | bytes accessed | tf_op | source)
XLA Modules:
  0.0 19.3 jit_solution(16296009847857538645)
XLA Ops:
  0.0 18.7 %paged_decode.1 = bf16[1,2,2048]{2,1,0:T(2,128)(2,1)S(1)} custom-call(bf16[1,2,2048]{2,1,0:T(2,128)(2,1)} %bitcast.7, bf16[1,2,128]{2,1,0:T(2,128)(2,1)} %bitcast.9, bf16[1,2,128]{2,1,0:T(2,128)(2,1)} %bitcast.10, s32[2,2,8]{2,1,0:T(2,128)} %bitcast.8, s32[1,2]{1,0:T(1,128)} %bitcast.11, bf16[64,128,128]{2,1,0:T(8,128)(2,1)} %k_hbm.1, ...), custom_call_target="tpu_custom_call" | custom-call | tf_op jit(solution)/shard_map/paged_decode/pallas_call | solution.py:374
  18.7 0.6 %copy.9 = bf16[2,1,2048]{2,0,1:T(2,128)(2,1)} copy(bf16[2,1,2048]{2,0,1:T(2,128)(2,1)S(1)} %bitcast.6) | data formatting | bytes 16384

commit v8 on v7

--- a/solution.py
+++ b/solution.py
@@ -147,8 +147,17 @@
         part = ref.at[pl.ds(0, count)]
         pltpu.make_async_copy(part, part, sem.at[which]).wait()
 
-    everyone(lambda there, other: send(meta_all.at[me], meta_all.at[me], 0, (there, other)))
-    holders(lambda there: send(q_all.at[rank], q_all.at[rank], 1, (there, shard)))
+    def tell(there, other):
+        send(meta_all.at[me], meta_all.at[me], 0, (there, other))
+
+    def ask(there):
+        send(q_all.at[rank], q_all.at[rank], 1, (there, shard))
+        for other in shard_at:
+            tell(there, other)
+
+    holders(ask)
+    for other in shard_at[1:]:
+        tell(rank, other)
 
     row_lane = within(iota((rows, LANES), 1), rows) == iota((rows, LANES), 0)
     spread_t = over(iota((slots, tall), 1), heads) == iota((slots, tall), 0)
@@ -309,8 +318,11 @@
 
     each_chunk(combine)
 
-    holders(lambda there: send(stat_out.at[there], stat_in.at[rank], 2, (there, shard)))
-    holders(lambda there: send(acc_out.at[there], acc_in.at[rank], 3, (there, shard)))
+    def answer(there):
+        send(stat_out.at[there], stat_in.at[rank], 2, (there, shard))
+        send(acc_out.at[there], acc_in.at[rank], 3, (there, shard))
+
+    holders(answer)
     stat_in[rank] = stat_out[rank]
     acc_in[rank] = acc_out[rank]
 

time: 19.5 us -> 20 us (1.026)
  Pallas kernels: 18.7 us -> 19.2 us
    pallas_call x1, Pallas kernels: 18.7 us -> 19.2 us  [per_device(): pl.pallas_call(partial(kernel, ranks, shards, micro, heads), out_shape=pl...]
where the time goes in v8:
time: 20 us; the launch traced here: 19.8 us
  Pallas kernels  19.2 us (96%)
  local copies, waits for them, and re-layouts  0.6 us (3%)
    pallas_call x1, Pallas kernels, per_device(): pl.pallas_call(partial(kernel, ranks, shards, micro, heads), out_shape=pl...  19.2 us
    unnamed x1, local copies, waits for them, and re-layouts  0.6 us

profile of v8, /device:TPU:0, one launch (start us, length us, event | category | flops | bytes accessed | tf_op | source)
XLA Modules:
  0.0 19.8 jit_solution(7074986930339836914)
XLA Ops:
  0.0 19.2 %paged_decode.1 = bf16[1,2,2048]{2,1,0:T(2,128)(2,1)S(1)} custom-call(bf16[1,2,2048]{2,1,0:T(2,128)(2,1)} %bitcast.7, bf16[1,2,128]{2,1,0:T(2,128)(2,1)} %bitcast.9, bf16[1,2,128]{2,1,0:T(2,128)(2,1)} %bitcast.10, s32[2,2,8]{2,1,0:T(2,128)} %bitcast.8, s32[1,2]{1,0:T(1,128)} %bitcast.11, bf16[64,128,128]{2,1,0:T(8,128)(2,1)} %k_hbm.1, ...), custom_call_target="tpu_custom_call" | custom-call | tf_op jit(solution)/shard_map/paged_decode/pallas_call | solution.py:386
  19.2 0.6 %copy.9 = bf16[2,1,2048]{2,0,1:T(2,128)(2,1)} copy(bf16[2,1,2048]{2,0,1:T(2,128)(2,1)S(1)} %bitcast.6) | data formatting | bytes 16384

commit v9 on v7

--- a/solution.py
+++ b/solution.py
@@ -98,7 +98,11 @@
     everyone(greet)
 
     def holders(body):
-        each(ranks - 1, lambda step: body(rank_at(step)))
+        if ranks < ROLLED_FROM:
+            for step in sorted(range(ranks - 1), key=lambda i: abs(i + 1 - ranks // 2)):
+                body(rank_at(step))
+        else:
+            each(ranks - 1, lambda step: body(rank_at(step)))
 
     lane = iota((1, LANES), 1)
     listed = list_vm.shape[2]

time: 19.5 us -> 19.7 us (1.010)
  Pallas kernels: 18.7 us -> 18.9 us
    pallas_call x1, Pallas kernels: 18.7 us -> 18.9 us  [per_device(): pl.pallas_call(partial(kernel, ranks, shards, micro, heads), out_shape=pl...]
where the time goes in v9:
time: 19.7 us; the launch traced here: 19.6 us
  Pallas kernels  18.9 us (96%)
  local copies, waits for them, and re-layouts  0.6 us (3%)
    pallas_call x1, Pallas kernels, per_device(): pl.pallas_call(partial(kernel, ranks, shards, micro, heads), out_shape=pl...  18.9 us
    unnamed x1, local copies, waits for them, and re-layouts  0.6 us

profile of v9, /device:TPU:0, one launch (start us, length us, event | category | flops | bytes accessed | tf_op | source)
XLA Modules:
  0.0 19.6 jit_solution(11762197660043175856)
XLA Ops:
  0.0 18.9 %paged_decode.1 = bf16[1,2,2048]{2,1,0:T(2,128)(2,1)S(1)} custom-call(bf16[1,2,2048]{2,1,0:T(2,128)(2,1)} %bitcast.7, bf16[1,2,128]{2,1,0:T(2,128)(2,1)} %bitcast.9, bf16[1,2,128]{2,1,0:T(2,128)(2,1)} %bitcast.10, s32[2,2,8]{2,1,0:T(2,128)} %bitcast.8, s32[1,2]{1,0:T(1,128)} %bitcast.11, bf16[64,128,128]{2,1,0:T(8,128)(2,1)} %k_hbm.1, ...), custom_call_target="tpu_custom_call" | custom-call | tf_op jit(solution)/shard_map/paged_decode/pallas_call | solution.py:378
  19.0 0.6 %copy.9 = bf16[2,1,2048]{2,0,1:T(2,128)(2,1)} copy(bf16[2,1,2048]{2,0,1:T(2,128)(2,1)S(1)} %bitcast.6) | data formatting | bytes 16384
